TPU v7x, 32 devices: a whole 2x2x4 slice. The times are simulated.
32 devices in a mesh: groups: 2 (over x), lat: 8 (over z, y), lon: 2 (over core).
Axes of the slice: x: 2, y: 2, z: 4, core: 2. Of those that a mesh axis runs over, the one named last changes fastest.
Arguments:
- grid_lat: bfloat16 [32768, 512], P(('groups', 'lat', 'lon')), parts along dimension 0, may hold values from -6 to 6
- mesh_lat: bfloat16 [8192, 512], P(('groups', 'lat', 'lon')), parts along dimension 0, may hold values from -6 to 6
- edge_lat: bfloat16 [49152, 512], P(('groups', 'lat', 'lon')), parts along dimension 0, may hold values from -6 to 6
- edge_src: int32 [49152], P(('groups', 'lat', 'lon')), parts along dimension 0, may hold values from 0 to 16383, as said below
- edge_dst: int32 [49152], P(('groups', 'lat', 'lon')), parts along dimension 0, may hold values from 0 to 4095, as said below
- edge_mask: int32 [49152], P(('groups', 'lat', 'lon')), parts along dimension 0, may hold values from 0 to 1, as said below
- grid_w1: bfloat16 [512, 512], replicated, may hold values from -0.25 to 0.25
- grid_w2: bfloat16 [512, 512], replicated, may hold values from -0.25 to 0.25
- edge_w_edge: bfloat16 [512, 512], replicated, may hold values from -0.15625 to 0.15625
- edge_w_grid: bfloat16 [512, 512], replicated, may hold values from -0.15625 to 0.15625
- edge_w_mesh: bfloat16 [512, 512], replicated, may hold values from -0.15625 to 0.15625
- edge_w2: bfloat16 [512, 512], replicated, may hold values from -0.25 to 0.25
- mesh_w1: bfloat16 [1024, 512], replicated, may hold values from -0.1875 to 0.1875
- mesh_w2: bfloat16 [512, 512], replicated, may hold values from -0.25 to 0.25
Outputs:
- mesh_out: bfloat16 [8192, 512], P(('groups', 'lat', 'lon')), parts along dimension 0
- grid_out: bfloat16 [32768, 512], P(('groups', 'lat', 'lon')), parts along dimension 0
There are 2 independent parts, one for each index of `groups`. A program takes and returns all parts, laid end to end along the dimension named above; an argument that names none is the same for every part. Nothing has to cross between parts.
Inputs may be any that keep to these rules, and one draw needn't show every extreme that they name: `edge_src`: the edge slots of device d (lat index i, lon index j, d = i * 2 + j) are slots d * 1536 to (d + 1) * 1536 - 1; each takes its source among device d's own grid nodes d * 1024 to (d + 1) * 1024 - 1, and every such grid node is the source of some slot of device d. `edge_dst`: an edge slot of a device with lat index i targets a mesh node of a device with lat index i - 1, i or i + 1 (either lon index). `edge_mask`: on each device the live slots come first, at least 512 of them; on some device all slots are live.
All inputs are finite; a program needn't handle non-finite values.
Results may differ from a plain program's by a relative error of at most 0.0057.
Values may be sent and summed in bfloat16 or wider, within the bound.
A program may use at most 64 MiB of HBM per device.

v0:
```python
import jax
import jax.numpy as jnp
from jax import lax
from jax.sharding import PartitionSpec as P


def with_halo(cells, sides, width):
    for axis, dim in sides:
        count = lax.axis_size(axis)
        ends = count - 1
        head = lax.slice_in_dim(cells, 0, width, axis=dim)
        tail = lax.slice_in_dim(cells, cells.shape[dim] - width, cells.shape[dim], axis=dim)
        cells = jnp.concatenate(
            [
                lax.ppermute(tail, axis, [(i, (i + 1) % count) for i in range(ends)]),
                cells,
                lax.ppermute(head, axis, [((i + 1) % count, i) for i in range(ends)]),
            ],
            axis=dim,
        )
    return cells


def passed_along(array, axis, by):
    peers = lax.axis_size(axis)
    pairs = [(i, i + by) for i in range(peers) if 0 <= i + by < peers]
    return lax.ppermute(array, axis, pairs)


def layer_norm(values):
    mean = jnp.mean(values, axis=-1, keepdims=True)
    centered = values - mean
    variance = jnp.mean(centered * centered, axis=-1, keepdims=True)
    return centered / jnp.sqrt(variance + 1e-05)


def per_device(
    grid_lat,
    mesh_lat,
    edge_lat,
    edge_src,
    edge_dst,
    edge_mask,
    grid_w1,
    grid_w2,
    edge_w_edge,
    edge_w_grid,
    edge_w_mesh,
    edge_w2,
    mesh_w1,
    mesh_w2,
):
    band = lax.axis_index("lat")
    column = lax.axis_index("lon")
    lon_count = lax.axis_size("lon")
    grid_rows = grid_lat.shape[0]
    mesh_rows = mesh_lat.shape[0]
    width = mesh_lat.shape[1]
    table_rows = 3 * lon_count * mesh_rows
    band_rows = lax.all_gather(mesh_lat, "lon", axis=0, tiled=True)
    table = with_halo(band_rows, (("lat", 0),), band_rows.shape[0])
    table_part = jnp.dot(table, edge_w_mesh, preferred_element_type=jnp.float32).astype(
        jnp.bfloat16
    )
    grid_mid = jax.nn.silu(jnp.dot(grid_lat, grid_w1, preferred_element_type=jnp.float32)).astype(
        jnp.bfloat16
    )
    grid_out = (
        grid_lat.astype(jnp.float32)
        + layer_norm(jnp.dot(grid_mid, grid_w2, preferred_element_type=jnp.float32))
    ).astype(jnp.bfloat16)
    grid_part = jnp.dot(grid_lat, edge_w_grid, preferred_element_type=jnp.float32).astype(
        jnp.bfloat16
    )
    local_src = edge_src - (band * lon_count + column) * grid_rows
    slots = edge_dst - (band - 1) * lon_count * mesh_rows
    edge_pre = jnp.dot(edge_lat, edge_w_edge, preferred_element_type=jnp.float32)
    edge_pre = edge_pre + jnp.take(grid_part, local_src, axis=0).astype(jnp.float32)
    edge_pre = edge_pre + jnp.take(table_part, slots, axis=0).astype(jnp.float32)
    edge_mid = jax.nn.silu(edge_pre).astype(jnp.bfloat16)
    edge_new = (
        edge_lat.astype(jnp.float32)
        + layer_norm(jnp.dot(edge_mid, edge_w2, preferred_element_type=jnp.float32))
    ).astype(jnp.bfloat16)
    positions = lax.broadcasted_iota(jnp.int32, (slots.shape[0], table_rows), 1)
    selector = ((slots[:, None] == positions) & (edge_mask[:, None] == 1)).astype(jnp.bfloat16)
    partial_sums = lax.dot_general(
        selector, edge_new, (((0,), (0,)), ((), ())), preferred_element_type=jnp.float32
    )
    blocks = partial_sums.reshape(3, lon_count * mesh_rows, width)
    from_above = passed_along(blocks[0], "lat", -1)
    from_below = passed_along(blocks[2].astype(jnp.bfloat16), "lat", 1).astype(jnp.float32)
    band_sum = blocks[1] + from_above + from_below
    agg = lax.psum_scatter(band_sum, "lon", scatter_dimension=0, tiled=True)
    agg_b = agg.astype(jnp.bfloat16)
    mesh_pre = jnp.dot(mesh_lat, mesh_w1[:width], preferred_element_type=jnp.float32) + jnp.dot(
        agg_b, mesh_w1[width:], preferred_element_type=jnp.float32
    )
    mesh_mid = jax.nn.silu(mesh_pre).astype(jnp.bfloat16)
    mesh_out = (
        mesh_lat.astype(jnp.float32)
        + layer_norm(jnp.dot(mesh_mid, mesh_w2, preferred_element_type=jnp.float32))
    ).astype(jnp.bfloat16)
    return (mesh_out, grid_out)


def solution(mesh):
    in_specs = (
        P(("groups", "lat", "lon"), None),
        P(("groups", "lat", "lon"), None),
        P(("groups", "lat", "lon"), None),
        P(("groups", "lat", "lon")),
        P(("groups", "lat", "lon")),
        P(("groups", "lat", "lon")),
        P(),
        P(),
        P(),
        P(),
        P(),
        P(),
        P(),
        P(),
    )
    out_specs = (P(("groups", "lat", "lon"), None), P(("groups", "lat", "lon"), None))
    return jax.shard_map(
        per_device, mesh=mesh, in_specs=in_specs, out_specs=out_specs, check_vma=False
    )
```

profile of v0, /device:TPU:8, one launch (start us, length us, event | category | flops | bytes accessed | tf_op | source)
XLA Modules:
  0.0 117.2 jit_solution(9082570226081198535)
XLA Ops:
  7.2 2.5 %all_gather.3 = bf16[512,512]{1,0:T(8,128)(2,1)S(1)} all-gather(bf16[256,512]{1,0:T(8,128)(2,1)} %param.15), channel_id=1, replica_groups=mesh['groups'=2,'lat'=8,'lon'=2] {'lon'}, dimensions={0}, use_global_device_ids=true | all-gather | bytes 786432 | tf_op jit(solution)/shard_map/all_gather | solution.py:60
  9.8 3.4 %collective-permute-start = (bf16[512,512]{1,0:T(8,128)(2,1)S(1)}, bf16[512,512]{1,0:T(8,128)(2,1)}, u32[]{:S(2)}, u32[]{:S(2)}) collective-permute-start(bf16[512,512]{1,0:T(8,128)(2,1)S(1)} %all_gather.3), channel_id=1, source_target_pairs={{0,2},{2,4},{4,6},{6,8},{8,10},{10,12},{12,14},{1,3},{3,5},{5,7},{... | collective-permute-start | bytes 1572872 | tf_op jit(solution)/shard_map/ppermute | solution.py:15
  13.2 3.3 %collective-permute-start.1 = (bf16[512,512]{1,0:T(8,128)(2,1)S(1)}, bf16[512,512]{1,0:T(8,128)(2,1)}, u32[]{:S(2)}, u32[]{:S(2)}) collective-permute-start(bf16[512,512]{1,0:T(8,128)(2,1)S(1)} %all_gather.3), channel_id=1, source_target_pairs={{2,0},{4,2},{6,4},{8,6},{10,8},{12,10},{14,12},{3,1},{5,3},{7,5},{... | collective-permute-start | bytes 1572872 | tf_op jit(solution)/shard_map/ppermute | solution.py:17
  17.3 2.6 %copy.16 = bf16[1536,512]{0,1:T(8,128)(2,1)} copy(bf16[1536,512]{1,0:T(8,128)(2,1)} %param.16) | data formatting | bytes 3145728 | tf_op args[2]
  19.9 1.7 %convolution_convert_fusion.1 = bf16[1024,512]{1,0:T(8,128)(2,1)S(1)} fusion(bf16[1024,512]{1,0:T(8,128)(2,1)S(1)} %copy-done.5, bf16[512,512]{1,0:T(8,128)(2,1)} %param.23), kind=kOutput, calls=%fused_computation.24 | convolution fusion | flops 537395200 | bytes 2621440 | tf_op jit(solution)/shard_map/dot_general | solution.py:72
  21.6 5.4 %gather_fusion = bf16[1536,512]{1,0:T(8,128)(2,1)} fusion(bf16[1024,512]{1,0:T(8,128)(2,1)S(1)} %convolution_convert_fusion.1, s32[2048]{0:T(1024)S(1)} %pad_clamp_fusion.1), kind=kCustom, calls=%fused_computation | custom fusion | bytes 3151872 | tf_op jit(solution)/shard_map/jit(_take)/gather | solution.py:78
  27.1 8.8 %collective-permute-done = bf16[512,512]{1,0:T(8,128)(2,1)} collective-permute-done((bf16[512,512]{1,0:T(8,128)(2,1)S(1)}, bf16[512,512]{1,0:T(8,128)(2,1)}, u32[]{:S(2)}, u32[]{:S(2)}) %collective-permute-start) | collective-permute-done | bytes 524320 | tf_op jit(solution)/shard_map/ppermute | solution.py:15
  35.9 2.0 %collective-permute-done.1 = bf16[512,512]{1,0:T(8,128)(2,1)} collective-permute-done((bf16[512,512]{1,0:T(8,128)(2,1)S(1)}, bf16[512,512]{1,0:T(8,128)(2,1)}, u32[]{:S(2)}, u32[]{:S(2)}) %collective-permute-start.1) | collective-permute-done | bytes 524320 | tf_op jit(solution)/shard_map/ppermute | solution.py:17
  37.9 2.5 %convolution_convert_fusion = bf16[1536,512]{1,0:T(8,128)(2,1)S(1)} fusion(bf16[512,512]{1,0:T(8,128)(2,1)} %param.24, bf16[512,512]{1,0:T(8,128)(2,1)} %collective-permute-done.1, bf16[512,512]{1,0:T(8,128)(2,1)} %copy-done.6, bf16[512,512]{1,0:T(8,128)(2,1)} %collective-permute-done), kind=kOutput, calls=%fused_computation.13 | convolution fusion | flops 810811392 | bytes 3670016 | tf_op jit(solution)/shard_map/dot_general | solution.py:62
  40.4 5.4 %gather_fusion.1 = bf16[1536,512]{1,0:T(8,128)(2,1)} fusion(bf16[1536,512]{1,0:T(8,128)(2,1)S(1)} %convolution_convert_fusion, s32[2048]{0:T(1024)S(1)} %pad_clamp_fusion), kind=kCustom, calls=%fused_computation.1 | custom fusion | bytes 3151872 | tf_op jit(solution)/shard_map/jit(_take)/gather | solution.py:79
  45.8 6.3 %fusion.31 = (f32[1536]{0:T(1024)S(1)}, f32[1536,512]{0,1:T(8,128)}) fusion(bf16[512,512]{1,0:T(8,128)(2,1)S(1)} %copy-done, bf16[1536,512]{1,0:T(8,128)(2,1)} %param.16, bf16[512,512]{1,0:T(8,128)(2,1)} %param.22, bf16[1536,512]{1,0:T(8,128)(2,1)} %gather_fusion.1, bf16[1536,512]{1,0:T(8,128)(2,1)} %gather_fusion, ...), kind=kOutput, calls=%fused_computation.60 | convolution fusion | flops 1620048384 | bytes 8922112 | tf_op jit(solution)/shard_map/dot_general | solution.py:83
  52.0 2.4 %multiply_reduce_fusion = f32[1536]{0:T(1024)S(1)} fusion(f32[1536,512]{0,1:T(8,128)} %get-tuple-element.9, f32[1536]{0:T(1024)S(1)} %broadcast_multiply_fusion), kind=kLoop, calls=%fused_computation.11 | loop fusion | flops 2357760 | bytes 3158016 | tf_op jit(solution)/shard_map/reduce_sum | solution.py:33
  54.9 3.2 %fusion.2 = f32[1536,512]{1,0:T(8,128)S(1)} fusion(s32[1536]{0:T(1024)S(1)} %get-tuple-element.7, pred[1536]{0:T(1024)(128)(4,1)S(1)} %broadcast_compare_fusion, bf16[1536,512]{0,1:T(8,128)(2,1)S(1)} %copy-done.4, f32[1536,512]{0,1:T(8,128)S(1)} %copy-done.2, f32[1536]{0:T(1024)S(1)} %add_sqrt_fusion, f32[1536]{0:T(1024)S(1)} %broadcast_multiply_fusion), kind=kOutput, calls=%fused_computation.5 | convolution fusion | flops 2426929152 | bytes 7884288 | tf_op jit(solution)/shard_map/dot_general | solution.py:87
  58.2 2.4 %collective-permute-start.2 = (f32[512,512]{1,0:T(8,128)S(1)}, f32[512,512]{1,0:T(8,128)S(1)}, u32[]{:S(2)}, u32[]{:S(2)}) collective-permute-start(f32[512,512]{1,0:T(8,128)S(1)} %slice.29), channel_id=1, source_target_pairs={{2,0},{4,2},{6,4},{8,6},{10,8},{12,10},{14,12},{3,1},{5,3},{7,5},{... | collective-permute-start | bytes 3145736 | tf_op jit(solution)/shard_map/ppermute | solution.py:27
  60.7 3.6 %collective-permute-start.3 = (bf16[512,512]{1,0:T(8,128)(2,1)S(1)}, bf16[512,512]{1,0:T(8,128)(2,1)S(1)}, u32[]{:S(2)}, u32[]{:S(2)}) collective-permute-start(bf16[512,512]{1,0:T(8,128)(2,1)S(1)} %slice.40), channel_id=1, source_target_pairs={{0,2},{2,4},{4,6},{6,8},{8,10},{10,12},{12,14},{1,3},{3,5},{5,7},{... | collective-permute-start | bytes 1572872 | tf_op jit(solution)/shard_map/ppermute | solution.py:27
  64.3 30.9 %collective-permute-done.3 = bf16[512,512]{1,0:T(8,128)(2,1)S(1)} collective-permute-done((bf16[512,512]{1,0:T(8,128)(2,1)S(1)}, bf16[512,512]{1,0:T(8,128)(2,1)S(1)}, u32[]{:S(2)}, u32[]{:S(2)}) %collective-permute-start.3) | collective-permute-done | bytes 524320 | tf_op jit(solution)/shard_map/ppermute | solution.py:27
  95.2 1.2 %collective-permute-done.2 = f32[512,512]{1,0:T(8,128)S(1)} collective-permute-done((f32[512,512]{1,0:T(8,128)S(1)}, f32[512,512]{1,0:T(8,128)S(1)}, u32[]{:S(2)}, u32[]{:S(2)}) %collective-permute-start.2) | collective-permute-done | bytes 1048608 | tf_op jit(solution)/shard_map/ppermute | solution.py:27
  96.4 1.3 %fusion.15 = f32[512,512]{1,0:T(8,128)} fusion(f32[512,512]{1,0:T(8,128)S(1)} %collective-permute-done.2, f32[1536,512]{1,0:T(8,128)S(1)} %fusion.2, bf16[512,512]{1,0:T(8,128)(2,1)S(1)} %collective-permute-done.3), kind=kLoop, calls=%fused_computation.29 | loop fusion | flops 786432 | bytes 3670016 | tf_op jit(solution)/shard_map/add | solution.py:93
  97.7 1.3 %copy.17 = bf16[1024,512]{0,1:T(8,128)(2,1)} copy(bf16[1024,512]{1,0:T(8,128)(2,1)S(1)} %copy-done.5) | data formatting | bytes 2097152 | tf_op args[0]
  99.0 3.0 %fusion.37 = (f32[1024]{0:T(1024)S(1)}, f32[1024,512]{0,1:T(8,128)S(1)}) fusion(bf16[512,512]{1,0:T(8,128)(2,1)} %param.21, bf16[1024,512]{1,0:T(8,128)(2,1)} %param.14, bf16[512,512]{1,0:T(8,128)(2,1)} %param.20), kind=kOutput, calls=%fused_computation.62 | convolution fusion | flops 1076886528 | bytes 4198400 | tf_op jit(solution)/shard_map/dot_general | solution.py:70
  102.4 0.9 copy-done.1
  103.3 1.5 %add_convert_fusion.1 = bf16[1024,512]{0,1:T(8,128)(2,1)} fusion(bf16[1024,512]{0,1:T(8,128)(2,1)S(1)} %copy-done.1, f32[1024,512]{0,1:T(8,128)S(1)} %get-tuple-element.13, f32[1024]{0:T(1024)S(1)} %add_sqrt_fusion.1, f32[1024]{0:T(1024)S(1)} %broadcast_multiply_fusion.1), kind=kLoop, calls=%fused_computation.14 | loop fusion | flops 2621440 | bytes 4202496 | tf_op jit(solution)/shard_map/convert_element_type | solution.py:71
  104.7 2.4 %copy.18 = bf16[1024,512]{1,0:T(8,128)(2,1)} copy(bf16[1024,512]{0,1:T(8,128)(2,1)} %add_convert_fusion.1) | data formatting | bytes 2097152
  107.5 1.7 %fusion.32 = (f32[256]{0:T(256)S(1)}, f32[256,512]{1,0:T(8,128)S(1)}) fusion(bf16[512,512]{1,0:T(8,128)(2,1)S(1)} %copy-done.9, f32[256,512]{1,0:T(8,128)S(1)} %fusion.21, bf16[1024,512]{1,0:T(8,128)(2,1)S(1)} %copy-done.7, f32[256,512]{1,0:T(8,128)} %reduce-scatter.2.cloned.1.call-done), kind=kOutput, calls=%fused_computation.61 | convolution fusion | flops 269483776 | bytes 2622464 | tf_op jit(solution)/shard_map/dot_general | solution.py:102
  (39 shorter events, 3.1 us)
Async XLA Ops:
  7.2 38.6 %copy-start = (bf16[512,512]{1,0:T(8,128)(2,1)S(1)}, bf16[512,512]{1,0:T(8,128)(2,1)}, u32[]{:S(2)}) copy-start(bf16[512,512]{1,0:T(8,128)(2,1)} %param.25) | copy-start | bytes 1572868
  7.2 12.7 %copy-start.5 = (bf16[1024,512]{1,0:T(8,128)(2,1)S(1)}, bf16[1024,512]{1,0:T(8,128)(2,1)}, u32[]{:S(2)}) copy-start(bf16[1024,512]{1,0:T(8,128)(2,1)} %param.14) | copy-start | bytes 3145732
  7.2 100.3 %reduce-scatter.2.cloned.1.call-start = ((), (), s32[]{:S(2)}) async-start(), calls=%async_computation.1 | async-start | bytes 1572864 | tf_op jit(solution)/shard_map/reduce_scatter | solution.py:94
  9.8 11.8 %copy-start.6 = (bf16[512,512]{1,0:T(8,128)(2,1)}, bf16[512,512]{1,0:T(8,128)(2,1)S(1)}, u32[]{:S(2)}) copy-start(bf16[512,512]{1,0:T(8,128)(2,1)S(1)} %all_gather.3) | copy-start | bytes 1572868
  9.8 26.1 %collective-permute-start = (bf16[512,512]{1,0:T(8,128)(2,1)S(1)}, bf16[512,512]{1,0:T(8,128)(2,1)}, u32[]{:S(2)}, u32[]{:S(2)}) collective-permute-start(bf16[512,512]{1,0:T(8,128)(2,1)S(1)} %all_gather.3), channel_id=1, source_target_pairs={{0,2},{2,4},{4,6},{6,8},{8,10},{10,12},{12,14},{1,3},{3,5},{5,7},{... | collective-permute-start | bytes 1572872 | tf_op jit(solution)/shard_map/ppermute | solution.py:15
  13.2 24.7 %collective-permute-start.1 = (bf16[512,512]{1,0:T(8,128)(2,1)S(1)}, bf16[512,512]{1,0:T(8,128)(2,1)}, u32[]{:S(2)}, u32[]{:S(2)}) collective-permute-start(bf16[512,512]{1,0:T(8,128)(2,1)S(1)} %all_gather.3), channel_id=1, source_target_pairs={{2,0},{4,2},{6,4},{8,6},{10,8},{12,10},{14,12},{3,1},{5,3},{7,5},{... | collective-permute-start | bytes 1572872 | tf_op jit(solution)/shard_map/ppermute | solution.py:17
  21.6 5.5 %copy-start.8 = (s32[1536]{0:T(1024)S(1)}, s32[1536]{0:T(1024)}, u32[]{:S(2)}) copy-start(s32[1536]{0:T(1024)} %param.19) | copy-start | bytes 18436
  45.8 8.7 %copy-start.4 = (bf16[1536,512]{0,1:T(8,128)(2,1)S(1)}, bf16[1536,512]{0,1:T(8,128)(2,1)}, u32[]{:S(2)}) copy-start(bf16[1536,512]{0,1:T(8,128)(2,1)} %copy.16) | copy-start | bytes 4718596
  52.0 2.8 %copy-start.2 = (f32[1536,512]{0,1:T(8,128)S(1)}, f32[1536,512]{0,1:T(8,128)}, u32[]{:S(2)}) copy-start(f32[1536,512]{0,1:T(8,128)} %get-tuple-element.9) | copy-start | bytes 9437188
  58.2 38.2 %collective-permute-start.2 = (f32[512,512]{1,0:T(8,128)S(1)}, f32[512,512]{1,0:T(8,128)S(1)}, u32[]{:S(2)}, u32[]{:S(2)}) collective-permute-start(f32[512,512]{1,0:T(8,128)S(1)} %slice.29), channel_id=1, source_target_pairs={{2,0},{4,2},{6,4},{8,6},{10,8},{12,10},{14,12},{3,1},{5,3},{7,5},{... | collective-permute-start | bytes 3145736 | tf_op jit(solution)/shard_map/ppermute | solution.py:27
  60.7 34.5 %collective-permute-start.3 = (bf16[512,512]{1,0:T(8,128)(2,1)S(1)}, bf16[512,512]{1,0:T(8,128)(2,1)S(1)}, u32[]{:S(2)}, u32[]{:S(2)}) collective-permute-start(bf16[512,512]{1,0:T(8,128)(2,1)S(1)} %slice.40), channel_id=1, source_target_pairs={{0,2},{2,4},{4,6},{6,8},{8,10},{10,12},{12,14},{1,3},{3,5},{5,7},{... | collective-permute-start | bytes 1572872 | tf_op jit(solution)/shard_map/ppermute | solution.py:27
  102.0 1.2 %copy-start.1 = (bf16[1024,512]{0,1:T(8,128)(2,1)S(1)}, bf16[1024,512]{0,1:T(8,128)(2,1)}, u32[]{:S(2)}) copy-start(bf16[1024,512]{0,1:T(8,128)(2,1)} %copy.17) | copy-start | bytes 3145732
  104.7 2.4 %copy-start.3 = (bf16[256,512]{1,0:T(8,128)(2,1)S(1)}, bf16[256,512]{1,0:T(8,128)(2,1)}, u32[]{:S(2)}) copy-start(bf16[256,512]{1,0:T(8,128)(2,1)} %param.15) | copy-start | bytes 786436
  104.7 2.4 %copy-start.7 = (bf16[1024,512]{1,0:T(8,128)(2,1)S(1)}, bf16[1024,512]{1,0:T(8,128)(2,1)}, u32[]{:S(2)}) copy-start(bf16[1024,512]{1,0:T(8,128)(2,1)} %param.26) | copy-start | bytes 3145732
  104.7 2.8 %copy-start.9 = (bf16[512,512]{1,0:T(8,128)(2,1)S(1)}, bf16[512,512]{1,0:T(8,128)(2,1)}, u32[]{:S(2)}) copy-start(bf16[512,512]{1,0:T(8,128)(2,1)} %param.27) | copy-start | bytes 1572868
Sparse Core Ops, SparseCore 0:
  97.8 8.9 reduce-scatter.1
where the time goes:
time: 118 us; the launch traced here: 117 us
  waiting for transfers between devices  42.9 us (36%)
  local copies, waits for them, and re-layouts  18.7 us (16%)
  matrix products  18.7 us (16%)
  between operations  14.2 us (12%)
  starting transfers between devices  12.8 us (11%)
  other arithmetic  7.32 us (6%)
  blocking collectives  2.52 us (2%)
    ppermute x2, waiting for transfers between devices, passed_along(): return lax.ppermute(array, axis, pairs)  32.1 us
    ppermute x1, waiting for transfers between devices, with_halo(): lax.ppermute(tail, axis, [(i, (i + 1) % count) for i in range(ends)])  8.78 us
    unnamed x23, local copies, waits for them, and re-layouts  7.68 us
    dot_general x1, matrix products, per_device(): jnp.dot(edge_mid, edge_w2, preferred_element_type=jnp.float32)  6.26 us
    ppermute x2, starting transfers between devices, passed_along(): return lax.ppermute(array, axis, pairs)  6.02 us
    gather x1, local copies, waits for them, and re-layouts, per_device(): jnp.take(grid_part, local_src, axis=0).astype(jnp.float32)  5.44 us
    gather x1, local copies, waits for them, and re-layouts, per_device(): jnp.take(table_part, slots, axis=0).astype(jnp.float32)  5.42 us
    ppermute x1, starting transfers between devices, with_halo(): lax.ppermute(tail, axis, [(i, (i + 1) % count) for i in range(ends)])  3.42 us
  transfers between devices with their start and end apart: 5, of which 4 were waited for; matrix products, arithmetic and copies ran while one was open for 17% of the time, Pallas kernels for 0%

commit v1 on v0

v1 whole, which is shorter than its diff:
```python
import functools

import jax
import jax.numpy as jnp
from jax import lax
from jax.experimental import pallas as pl
from jax.experimental.pallas import tpu as pltpu
from jax.sharding import PartitionSpec as P

TILE = 256
CHUNKS = 2
MESH = pl.DeviceIdType.MESH


def silu(v):
    half = 0.5 * v
    return half + half * jnp.tanh(half)


def layer_norm(values):
    mean = jnp.mean(values, axis=-1, keepdims=True)
    centered = values - mean
    variance = jnp.mean(centered * centered, axis=-1, keepdims=True)
    return centered * lax.rsqrt(variance + 1e-05)


def dot(a, b):
    return jnp.dot(a, b, preferred_element_type=jnp.float32)


def spread(ref, tile):
    parts = []
    for k in range(TILE // 128):
        row = ref[pl.ds(tile * (TILE // 128) + k, 1), :]
        parts.append(jnp.broadcast_to(row, (128, 128)).T)
    return jnp.concatenate(parts, axis=0)


def picks(cols, bases, width):
    lanes = lax.broadcasted_iota(jnp.int32, (TILE, 128), 1)
    parts = []
    for base in bases:
        for k in range(width // 128):
            hit = cols == lanes + (base + 128 * k)
            parts.append(jnp.where(hit, 1.0, 0.0).astype(jnp.bfloat16))
    return jnp.concatenate(parts, axis=1)


def rows_of(tile):
    return pl.ds(pl.multiple_of(tile * TILE, TILE), TILE)


def kernel(
    lat_n,
    src_ref,
    dst_ref,
    mask_ref,
    grid_hbm,
    mesh_hbm,
    edge_hbm,
    gw1_hbm,
    gw2_hbm,
    wee_hbm,
    weg_hbm,
    wem_hbm,
    ew2_hbm,
    mw1_hbm,
    mw2_hbm,
    mesh_out,
    grid_out,
    grid,
    mesh,
    edge,
    gw1,
    gw2,
    wee,
    weg,
    wem,
    ew2,
    mw1,
    mw2,
    own,
    halo,
    part,
    pre,
    cols,
    live,
    fresh,
    gout,
    mout,
    pout,
    pin,
    acc,
    send,
    recv,
    mpre,
    in_sem,
    out_sem,
    own_sems,
    halo_send,
    halo_recv,
    fwd_send,
    fwd_recv,
    swap_send,
    swap_recv,
    msg_send,
    msg_recv,
):
    band = lax.axis_index("lat")
    col = lax.axis_index("lon")
    peer = 1 - col
    width = mesh.shape[1]
    mesh_rows = mesh.shape[0]
    grid_rows = grid.shape[0]
    slots_n = edge.shape[0]
    tiles = slots_n // TILE
    piece = mesh_rows // CHUNKS

    order = [
        (mesh_hbm, mesh),
        (wem_hbm, wem),
        (grid_hbm, grid),
        (weg_hbm, weg),
        (edge_hbm, edge),
        (wee_hbm, wee),
        (ew2_hbm, ew2),
        (gw1_hbm, gw1),
        (gw2_hbm, gw2),
        (mw1_hbm, mw1),
        (mw2_hbm, mw2),
    ]
    loads = [
        pltpu.make_async_copy(a, b, in_sem.at[i]) for i, (a, b) in enumerate(order)
    ]
    for load in loads:
        load.start()

    has = [band > 0, band < lat_n - 1]
    toward = [band - 1, band + 1]
    barrier = pltpu.get_barrier_semaphore()
    pl.semaphore_signal(barrier, inc=1, device_id={"lon": peer}, device_id_type=MESH)
    for side in range(2):

        @pl.when(has[side])
        def _():
            pl.semaphore_signal(
                barrier, inc=1, device_id={"lat": toward[side]}, device_id_type=MESH
            )

        @pl.when(jnp.logical_not(has[side]))
        def _():
            for q in range(CHUNKS):
                halo[q, 2 * side] = jnp.zeros((piece, width), jnp.bfloat16)
                halo[q, 2 * side + 1] = jnp.zeros((piece, width), jnp.bfloat16)

    loads[0].wait()
    loads[1].wait()
    own[col] = dot(mesh[...], wem[...]).astype(jnp.bfloat16)

    peers = 1 + jnp.minimum(band, 1) + jnp.minimum(lat_n - 1 - band, 1)
    pl.semaphore_wait(barrier, peers)

    def halo_copy(q, side):
        return pltpu.make_async_remote_copy(
            src_ref=own.at[col, pl.ds(q * piece, piece)],
            dst_ref=halo.at[q, 2 * (1 - side) + col],
            send_sem=halo_send.at[q, side],
            recv_sem=halo_recv.at[q, 1 - side],
            device_id={"lat": toward[side]},
            device_id_type=MESH,
        )

    def halo_arrival(q, side):
        return pltpu.make_async_remote_copy(
            src_ref=own.at[col, pl.ds(q * piece, piece)],
            dst_ref=halo.at[q, 2 * side + col],
            send_sem=halo_send.at[q, side],
            recv_sem=halo_recv.at[q, side],
            device_id={"lat": toward[side]},
            device_id_type=MESH,
        )

    def fwd_copy(q, side):
        return pltpu.make_async_remote_copy(
            src_ref=halo.at[q, 2 * side + col],
            dst_ref=halo.at[q, 2 * side + col],
            send_sem=fwd_send.at[q, side],
            recv_sem=fwd_recv.at[q, side],
            device_id={"lon": peer},
            device_id_type=MESH,
        )

    def fwd_arrival(q, side):
        return pltpu.make_async_remote_copy(
            src_ref=halo.at[q, 2 * side + col],
            dst_ref=halo.at[q, 2 * side + peer],
            send_sem=fwd_send.at[q, side],
            recv_sem=fwd_recv.at[q, side],
            device_id={"lon": peer},
            device_id_type=MESH,
        )

    for q in range(CHUNKS):
        for side in range(2):

            @pl.when(has[side])
            def _():
                halo_copy(q, side).start()

    own_copy = pltpu.make_async_remote_copy(
        src_ref=own.at[col],
        dst_ref=own.at[col],
        send_sem=own_sems.at[0],
        recv_sem=own_sems.at[1],
        device_id={"lon": peer},
        device_id_type=MESH,
    )
    own_copy.start()

    loads[2].wait()
    loads[3].wait()

    def grid_part(t, carry):
        rows = rows_of(t)
        part[rows, :] = dot(grid[rows, :], weg[...]).astype(jnp.bfloat16)
        return carry

    lax.fori_loop(0, grid_rows // TILE, grid_part, 0)

    loads[4].wait()
    loads[5].wait()
    pltpu.make_async_remote_copy(
        src_ref=own.at[col],
        dst_ref=own.at[peer],
        send_sem=own_sems.at[0],
        recv_sem=own_sems.at[1],
        device_id={"lon": peer},
        device_id_type=MESH,
    ).wait_recv()
    first_grid = (band * 2 + col) * grid_rows
    first_mesh = (band - 1) * 2 * mesh_rows
    live[...] = jnp.where(mask_ref[...] == 1, dst_ref[...] - first_mesh, -1)

    def before_halo(t, carry):
        rows = rows_of(t)
        source = spread(src_ref, t)
        target = spread(dst_ref, t) - first_mesh
        cols[rows, :] = target
        total = dot(edge[rows, :], wee[...])
        total += dot(picks(source, [first_grid], grid_rows), part[...])
        total += dot(
            picks(target, [2 * mesh_rows], 2 * mesh_rows),
            own[...].reshape(2 * mesh_rows, width),
        )
        pre[rows, :] = total
        return carry

    lax.fori_loop(0, tiles, before_halo, 0)

    def from_halo(q, target):
        bases = [
            2 * side * 2 * mesh_rows + c * mesh_rows + q * piece
            for side in range(2)
            for c in range(2)
        ]
        return dot(picks(target, bases, piece), halo[q].reshape(4 * piece, width))

    for q in range(CHUNKS):
        for side in range(2):

            @pl.when(has[side])
            def _():
                halo_arrival(q, side).wait_recv()
                fwd_copy(q, side).start()

        for side in range(2):

            @pl.when(has[side])
            def _():
                fwd_arrival(q, side).wait_recv()

        if q < CHUNKS - 1:

            def add_halo(t, carry):
                rows = rows_of(t)
                pre[rows, :] += from_halo(q, cols[rows, :])
                return carry

            lax.fori_loop(0, tiles, add_halo, 0)

    loads[6].wait()

    def edge_mlp(t, carry):
        rows = rows_of(t)
        total = pre[rows, :] + from_halo(CHUNKS - 1, cols[rows, :])
        mid = silu(total).astype(jnp.bfloat16)
        normed = layer_norm(dot(mid, ew2[...]))
        fresh[rows, :] = (edge[rows, :].astype(jnp.float32) + normed).astype(jnp.bfloat16)
        return carry

    lax.fori_loop(0, tiles, edge_mlp, 0)

    def sums(first):
        ids = lax.broadcasted_iota(jnp.int32, (mesh_rows, 128), 0) + first
        parts = []
        for k in range(slots_n // 128):
            hit = jnp.broadcast_to(live[k : k + 1, :], (mesh_rows, 128)) == ids
            parts.append(jnp.where(hit, 1.0, 0.0).astype(jnp.bfloat16))
        return dot(jnp.concatenate(parts, axis=1), fresh[...])

    def swap(i):
        return pltpu.make_async_remote_copy(
            src_ref=pout.at[i],
            dst_ref=pin.at[i],
            send_sem=swap_send.at[i],
            recv_sem=swap_recv.at[i],
            device_id={"lon": peer},
            device_id_type=MESH,
        )

    def message(side):
        return pltpu.make_async_remote_copy(
            src_ref=send.at[side],
            dst_ref=recv.at[side],
            send_sem=msg_send.at[side],
            recv_sem=msg_recv.at[side],
            device_id={"lat": toward[side]},
            device_id_type=MESH,
        )

    def block_first(block, c):
        return (block * 2 + c) * mesh_rows

    for side in range(2):
        pout[side] = sums(block_first(2 * side, peer))
        swap(side).start()
    for side in range(2):
        acc[...] = sums(block_first(2 * side, col))
        swap(side).wait_recv()
        send[side] = (acc[...] + pin[side]).astype(jnp.bfloat16)

        @pl.when(has[side])
        def _():
            message(side).start()

    pout[2] = sums(block_first(1, peer))
    swap(2).start()
    acc[...] = sums(block_first(1, col))

    for i in (7, 8, 9, 10):
        loads[i].wait()

    def grid_mlp(t, carry):
        rows = rows_of(t)
        mid = silu(dot(grid[rows, :], gw1[...])).astype(jnp.bfloat16)
        normed = layer_norm(dot(mid, gw2[...]))
        gout[rows, :] = (grid[rows, :].astype(jnp.float32) + normed).astype(jnp.bfloat16)
        return carry

    lax.fori_loop(0, grid_rows // TILE, grid_mlp, 0)
    store_grid = pltpu.make_async_copy(gout, grid_out, out_sem.at[0])
    store_grid.start()

    mpre[...] = dot(mesh[...], mw1[:width, :])
    swap(2).wait_recv()
    acc[...] += pin[2]
    for side in range(2):

        @pl.when(has[1 - side])
        def _():
            message(side).wait_recv()
            acc[...] += recv[side].astype(jnp.float32)

    mid = silu(mpre[...] + dot(acc[...].astype(jnp.bfloat16), mw1[width:, :])).astype(
        jnp.bfloat16
    )
    normed = layer_norm(dot(mid, mw2[...]))
    mout[...] = (mesh[...].astype(jnp.float32) + normed).astype(jnp.bfloat16)
    store_mesh = pltpu.make_async_copy(mout, mesh_out, out_sem.at[1])
    store_mesh.start()

    own_copy.wait_send()
    for i in range(3):
        swap(i).wait_send()
    for side in range(2):

        @pl.when(has[side])
        def _():
            message(side).wait_send()
            for q in range(CHUNKS):
                halo_copy(q, side).wait_send()
                fwd_copy(q, side).wait_send()

    store_grid.wait()
    store_mesh.wait()


def per_device(lat_n, *args):
    (grid_lat, mesh_lat, edge_lat, edge_src, edge_dst, edge_mask) = args[:6]
    weights = args[6:]
    width = mesh_lat.shape[1]
    mesh_rows = mesh_lat.shape[0]
    grid_rows = grid_lat.shape[0]
    slots = edge_lat.shape[0]
    bf16, f32 = jnp.bfloat16, jnp.float32
    piece = mesh_rows // CHUNKS
    dma = pltpu.SemaphoreType.DMA
    vmem = pltpu.VMEM
    scratch = [
        vmem(grid_lat.shape, bf16),
        vmem(mesh_lat.shape, bf16),
        vmem(edge_lat.shape, bf16),
        *[vmem(w.shape, bf16) for w in weights],
        vmem((2, mesh_rows, width), bf16),
        vmem((CHUNKS, 4, piece, width), bf16),
        vmem((grid_rows, width), bf16),
        vmem((slots, width), f32),
        vmem((slots, 128), jnp.int32),
        vmem((slots // 128, 128), jnp.int32),
        vmem((slots, width), bf16),
        vmem((grid_rows, width), bf16),
        vmem((mesh_rows, width), bf16),
        vmem((3, mesh_rows, width), f32),
        vmem((3, mesh_rows, width), f32),
        vmem((mesh_rows, width), f32),
        vmem((2, mesh_rows, width), bf16),
        vmem((2, mesh_rows, width), bf16),
        vmem((mesh_rows, width), f32),
        dma((11,)),
        dma((2,)),
        dma((2,)),
        dma((CHUNKS, 2)),
        dma((CHUNKS, 2)),
        dma((CHUNKS, 2)),
        dma((CHUNKS, 2)),
        dma((3,)),
        dma((3,)),
        dma((2,)),
        dma((2,)),
    ]
    in_vmem = pl.BlockSpec(memory_space=pltpu.VMEM)
    anywhere = pl.BlockSpec(memory_space=pl.ANY)
    return pl.pallas_call(
        functools.partial(kernel, lat_n),
        out_shape=(
            jax.ShapeDtypeStruct(mesh_lat.shape, bf16),
            jax.ShapeDtypeStruct(grid_lat.shape, bf16),
        ),
        in_specs=[in_vmem] * 3 + [anywhere] * 11,
        out_specs=(anywhere, anywhere),
        scratch_shapes=scratch,
        compiler_params=pltpu.CompilerParams(
            collective_id=0, has_side_effects=True, vmem_limit_bytes=48 * 2**20
        ),
    )(
        *[a.reshape(slots // 128, 128) for a in (edge_src, edge_dst, edge_mask)],
        grid_lat,
        mesh_lat,
        edge_lat,
        *weights,
    )


def solution(mesh):
    rows = P(("groups", "lat", "lon"), None)
    line = P(("groups", "lat", "lon"))
    return jax.shard_map(
        functools.partial(per_device, mesh.shape["lat"]),
        mesh=mesh,
        in_specs=(rows,) * 3 + (line,) * 3 + (P(),) * 8,
        out_specs=(rows, rows),
        check_vma=False,
    )
```

time: 118 us -> 51.8 us (0.44)
  waiting for transfers between devices: 42.9 us -> 0 us
  Pallas kernels: 0 us -> 38.3 us
  matrix products: 18.7 us -> 0 us
  between operations: 14.2 us -> 0.66 us
  starting transfers between devices: 12.8 us -> 0 us
  other arithmetic: 7.32 us -> 0 us
  local copies, waits for them, and re-layouts: 18.7 us -> 12 us
  blocking collectives: 2.52 us -> 0 us
    ppermute x4 -> x0, waiting for transfers between devices: 42.8 us -> none  [the longest x2 32.1 us: passed_along(): return lax.ppermute(array, axis, pairs)]
    pallas_call x0 -> x1, Pallas kernels: none -> 38.3 us  [per_device(): pl.pallas_call(functools.partial(kernel, lat_n), out_shape=(jax.ShapeDtyp...]
    dot_general x7 -> x0, matrix products: 18.7 us -> none  [the longest x1 6.26 us: per_device(): jnp.dot(edge_mid, edge_w2, preferred_element_type=jnp.float32)]
    ppermute x4 -> x0, starting transfers between devices: 12.8 us -> none  [the longest x2 6.02 us: passed_along(): return lax.ppermute(array, axis, pairs)]
    gather x2 -> x0, local copies, waits for them, and re-layouts: 10.9 us -> none  [the longest x1 5.44 us: per_device(): jnp.take(grid_part, local_src, axis=0).astype(jnp.float32)]
    unnamed x23 -> x24, local copies, waits for them, and re-layouts: 7.68 us -> 12 us
    reduce_sum x3 -> x0, other arithmetic: 2.89 us -> none  [layer_norm(): variance = jnp.mean(centered * centered, axis=-1, keepdims=True)]
    all_gather x1 -> x0, blocking collectives: 2.52 us -> none  [per_device(): band_rows = lax.all_gather(mesh_lat, 'lon', axis=0, tiled=True)]
  transfers between devices with their start and end apart: 5 -> 0, of which waited for: 4 -> 0; matrix products, arithmetic and copies ran while one was open for 17% -> 0% of each run, Pallas kernels for 0% -> 0%
where the time goes in v1:
time: 51.8 us; the launch traced here: 50.9 us
  Pallas kernels  38.3 us (74%)
  local copies, waits for them, and re-layouts  12 us (23%)
  between operations  0.66 us (1%)
    pallas_call x1, Pallas kernels, per_device(): pl.pallas_call(functools.partial(kernel, lat_n), out_shape=(jax.ShapeDtyp...  38.3 us
    unnamed x24, local copies, waits for them, and re-layouts  12 us

profile of v1, /device:TPU:8, one launch (start us, length us, event | category | flops | bytes accessed | tf_op | source)
XLA Modules:
  0.0 50.9 jit_solution(6617793149305441353)
XLA Ops:
  0.6 0.0 copy-start
  0.6 1.0 %copy-done = bf16[512,512]{1,0:T(8,128)(2,1)S(1)} copy-done((bf16[512,512]{1,0:T(8,128)(2,1)S(1)}, bf16[512,512]{1,0:T(8,128)(2,1)}, u32[]{:S(2)}) %copy-start) | copy-done | bytes 524312
  1.7 0.0 copy-start.1
  1.7 1.0 %copy-done.1 = bf16[512,512]{1,0:T(8,128)(2,1)S(1)} copy-done((bf16[512,512]{1,0:T(8,128)(2,1)S(1)}, bf16[512,512]{1,0:T(8,128)(2,1)}, u32[]{:S(2)}) %copy-start.1) | copy-done | bytes 524312
  2.7 0.0 copy-start.2
  2.7 1.0 %copy-done.2 = bf16[512,512]{1,0:T(8,128)(2,1)S(1)} copy-done((bf16[512,512]{1,0:T(8,128)(2,1)S(1)}, bf16[512,512]{1,0:T(8,128)(2,1)}, u32[]{:S(2)}) %copy-start.2) | copy-done | bytes 524312
  3.8 0.0 copy-start.3
  3.8 1.0 %copy-done.3 = bf16[512,512]{1,0:T(8,128)(2,1)S(1)} copy-done((bf16[512,512]{1,0:T(8,128)(2,1)S(1)}, bf16[512,512]{1,0:T(8,128)(2,1)}, u32[]{:S(2)}) %copy-start.3) | copy-done | bytes 524312
  4.8 0.0 copy-start.4
  4.8 1.0 %copy-done.4 = bf16[512,512]{1,0:T(8,128)(2,1)S(1)} copy-done((bf16[512,512]{1,0:T(8,128)(2,1)S(1)}, bf16[512,512]{1,0:T(8,128)(2,1)}, u32[]{:S(2)}) %copy-start.4) | copy-done | bytes 524312
  5.8 0.0 copy-start.5
  5.8 1.0 %copy-done.5 = bf16[512,512]{1,0:T(8,128)(2,1)S(1)} copy-done((bf16[512,512]{1,0:T(8,128)(2,1)S(1)}, bf16[512,512]{1,0:T(8,128)(2,1)}, u32[]{:S(2)}) %copy-start.5) | copy-done | bytes 524312
  6.9 0.0 copy-start.6
  6.9 1.0 %copy-done.6 = bf16[512,512]{1,0:T(8,128)(2,1)S(1)} copy-done((bf16[512,512]{1,0:T(8,128)(2,1)S(1)}, bf16[512,512]{1,0:T(8,128)(2,1)}, u32[]{:S(2)}) %copy-start.6) | copy-done | bytes 524312
  7.9 0.9 %copy-done.7 = bf16[256,512]{1,0:T(8,128)(2,1)S(1)} copy-done((bf16[256,512]{1,0:T(8,128)(2,1)S(1)}, bf16[256,512]{1,0:T(8,128)(2,1)}, u32[]{:S(2)}) %copy-start.7) | copy-done | bytes 262168
  8.9 0.0 copy-start.8
  8.9 0.7 %copy-done.8 = s32[1536]{0:T(1024)S(1)} copy-done((s32[1536]{0:T(1024)S(1)}, s32[1536]{0:T(1024)}, u32[]{:S(2)}) %copy-start.8) | copy-done | bytes 6168
  9.6 0.0 copy-start.9
  9.6 0.7 %copy-done.9 = s32[1536]{0:T(1024)S(1)} copy-done((s32[1536]{0:T(1024)S(1)}, s32[1536]{0:T(1024)}, u32[]{:S(2)}) %copy-start.9) | copy-done | bytes 6168
  10.3 0.0 copy-start.10
  10.3 0.7 %copy-done.10 = s32[1536]{0:T(1024)S(1)} copy-done((s32[1536]{0:T(1024)S(1)}, s32[1536]{0:T(1024)}, u32[]{:S(2)}) %copy-start.10) | copy-done | bytes 6168
  11.0 38.3 %shard_map.149 = (bf16[256,512]{1,0:T(8,128)(2,1)S(1)}, bf16[1024,512]{1,0:T(8,128)(2,1)S(1)}) custom-call(s32[12,128]{1,0:T(8,128)S(1)} %bitcast.3, s32[12,128]{1,0:T(8,128)S(1)} %bitcast.4, s32[12,128]{1,0:T(8,128)S(1)} %bitcast.5, bf16[1024,512]{1,0:T(8,128)(2,1)} %grid_hbm.1, bf16[256,512]{1,0:T(8,128)(2,1)S(1)} %copy-done.7, ...), custom_call_target="tpu_custom_call" | custom-call | tf_op jit(solution)/shard_map/pallas_call | solution.py:443
  49.3 0.7 %copy.18 = bf16[256,512]{1,0:T(8,128)(2,1)} copy(bf16[256,512]{1,0:T(8,128)(2,1)S(1)} %get-tuple-element.4) | data formatting | bytes 524288
  50.0 1.0 %copy.19 = bf16[1024,512]{1,0:T(8,128)(2,1)} copy(bf16[1024,512]{1,0:T(8,128)(2,1)S(1)} %get-tuple-element.5) | data formatting | bytes 2097152
  (1 shorter events, 0.0 us)
Async XLA Ops:
  0.6 1.0 %copy-start = (bf16[512,512]{1,0:T(8,128)(2,1)S(1)}, bf16[512,512]{1,0:T(8,128)(2,1)}, u32[]{:S(2)}) copy-start(bf16[512,512]{1,0:T(8,128)(2,1)} %gw1_hbm.1) | copy-start | bytes 1572868
  1.7 1.0 %copy-start.1 = (bf16[512,512]{1,0:T(8,128)(2,1)S(1)}, bf16[512,512]{1,0:T(8,128)(2,1)}, u32[]{:S(2)}) copy-start(bf16[512,512]{1,0:T(8,128)(2,1)} %gw2_hbm.1) | copy-start | bytes 1572868
  2.7 1.0 %copy-start.2 = (bf16[512,512]{1,0:T(8,128)(2,1)S(1)}, bf16[512,512]{1,0:T(8,128)(2,1)}, u32[]{:S(2)}) copy-start(bf16[512,512]{1,0:T(8,128)(2,1)} %wee_hbm.1) | copy-start | bytes 1572868
  3.8 1.0 %copy-start.3 = (bf16[512,512]{1,0:T(8,128)(2,1)S(1)}, bf16[512,512]{1,0:T(8,128)(2,1)}, u32[]{:S(2)}) copy-start(bf16[512,512]{1,0:T(8,128)(2,1)} %weg_hbm.1) | copy-start | bytes 1572868
  4.8 1.0 %copy-start.4 = (bf16[512,512]{1,0:T(8,128)(2,1)S(1)}, bf16[512,512]{1,0:T(8,128)(2,1)}, u32[]{:S(2)}) copy-start(bf16[512,512]{1,0:T(8,128)(2,1)} %wem_hbm.1) | copy-start | bytes 1572868
  5.8 1.0 %copy-start.5 = (bf16[512,512]{1,0:T(8,128)(2,1)S(1)}, bf16[512,512]{1,0:T(8,128)(2,1)}, u32[]{:S(2)}) copy-start(bf16[512,512]{1,0:T(8,128)(2,1)} %ew2_hbm.1) | copy-start | bytes 1572868
  6.9 1.0 %copy-start.6 = (bf16[512,512]{1,0:T(8,128)(2,1)S(1)}, bf16[512,512]{1,0:T(8,128)(2,1)}, u32[]{:S(2)}) copy-start(bf16[512,512]{1,0:T(8,128)(2,1)} %mw2_hbm.1) | copy-start | bytes 1572868
  7.9 0.9 %copy-start.7 = (bf16[256,512]{1,0:T(8,128)(2,1)S(1)}, bf16[256,512]{1,0:T(8,128)(2,1)}, u32[]{:S(2)}) copy-start(bf16[256,512]{1,0:T(8,128)(2,1)} %mesh_hbm.1) | copy-start | bytes 786436
  8.9 0.7 %copy-start.8 = (s32[1536]{0:T(1024)S(1)}, s32[1536]{0:T(1024)}, u32[]{:S(2)}) copy-start(s32[1536]{0:T(1024)} %param.17) | copy-start | bytes 18436
  9.6 0.7 %copy-start.9 = (s32[1536]{0:T(1024)S(1)}, s32[1536]{0:T(1024)}, u32[]{:S(2)}) copy-start(s32[1536]{0:T(1024)} %param.18) | copy-start | bytes 18436
  10.3 0.7 %copy-start.10 = (s32[1536]{0:T(1024)S(1)}, s32[1536]{0:T(1024)}, u32[]{:S(2)}) copy-start(s32[1536]{0:T(1024)} %param.19) | copy-start | bytes 18436

commit v2 on v1

--- a/solution.py
+++ b/solution.py
@@ -9,6 +9,7 @@
 
 TILE = 256
 CHUNKS = 2
+VMEM_BYTES = 63 * 2**20
 MESH = pl.DeviceIdType.MESH
 
 
@@ -132,7 +133,7 @@
     loads = [
         pltpu.make_async_copy(a, b, in_sem.at[i]) for i, (a, b) in enumerate(order)
     ]
-    for load in loads:
+    for load in loads[:2]:
         load.start()
 
     has = [band > 0, band < lat_n - 1]
@@ -149,12 +150,12 @@
 
         @pl.when(jnp.logical_not(has[side]))
         def _():
-            for q in range(CHUNKS):
-                halo[q, 2 * side] = jnp.zeros((piece, width), jnp.bfloat16)
-                halo[q, 2 * side + 1] = jnp.zeros((piece, width), jnp.bfloat16)
+            halo[side] = jnp.zeros((2, mesh_rows, width), jnp.bfloat16)
 
     loads[0].wait()
     loads[1].wait()
+    for load in loads[2:]:
+        load.start()
     own[col] = dot(mesh[...], wem[...]).astype(jnp.bfloat16)
 
     peers = 1 + jnp.minimum(band, 1) + jnp.minimum(lat_n - 1 - band, 1)
@@ -163,7 +164,7 @@
     def halo_copy(q, side):
         return pltpu.make_async_remote_copy(
             src_ref=own.at[col, pl.ds(q * piece, piece)],
-            dst_ref=halo.at[q, 2 * (1 - side) + col],
+            dst_ref=halo.at[1 - side, col, pl.ds(q * piece, piece)],
             send_sem=halo_send.at[q, side],
             recv_sem=halo_recv.at[q, 1 - side],
             device_id={"lat": toward[side]},
@@ -173,7 +174,7 @@
     def halo_arrival(q, side):
         return pltpu.make_async_remote_copy(
             src_ref=own.at[col, pl.ds(q * piece, piece)],
-            dst_ref=halo.at[q, 2 * side + col],
+            dst_ref=halo.at[side, col, pl.ds(q * piece, piece)],
             send_sem=halo_send.at[q, side],
             recv_sem=halo_recv.at[q, side],
             device_id={"lat": toward[side]},
@@ -182,8 +183,8 @@
 
     def fwd_copy(q, side):
         return pltpu.make_async_remote_copy(
-            src_ref=halo.at[q, 2 * side + col],
-            dst_ref=halo.at[q, 2 * side + col],
+            src_ref=halo.at[side, col, pl.ds(q * piece, piece)],
+            dst_ref=halo.at[side, col, pl.ds(q * piece, piece)],
             send_sem=fwd_send.at[q, side],
             recv_sem=fwd_recv.at[q, side],
             device_id={"lon": peer},
@@ -192,21 +193,21 @@
 
     def fwd_arrival(q, side):
         return pltpu.make_async_remote_copy(
-            src_ref=halo.at[q, 2 * side + col],
-            dst_ref=halo.at[q, 2 * side + peer],
+            src_ref=halo.at[side, col, pl.ds(q * piece, piece)],
+            dst_ref=halo.at[side, peer, pl.ds(q * piece, piece)],
             send_sem=fwd_send.at[q, side],
             recv_sem=fwd_recv.at[q, side],
             device_id={"lon": peer},
             device_id_type=MESH,
         )
 
-    for q in range(CHUNKS):
-        for side in range(2):
-
-            @pl.when(has[side])
-            def _():
+    def send_halo(side):
+        @pl.when(has[side])
+        def _():
+            for q in range(CHUNKS):
                 halo_copy(q, side).start()
 
+    send_halo(1)
     own_copy = pltpu.make_async_remote_copy(
         src_ref=own.at[col],
         dst_ref=own.at[col],
@@ -257,48 +258,32 @@
 
     lax.fori_loop(0, tiles, before_halo, 0)
 
-    def from_halo(q, target):
-        bases = [
-            2 * side * 2 * mesh_rows + c * mesh_rows + q * piece
-            for side in range(2)
-            for c in range(2)
-        ]
-        return dot(picks(target, bases, piece), halo[q].reshape(4 * piece, width))
-
-    for q in range(CHUNKS):
-        for side in range(2):
-
-            @pl.when(has[side])
-            def _():
+    send_halo(0)
+    loads[6].wait()
+
+    def receive_halo(side):
+        @pl.when(has[side])
+        def _():
+            for q in range(CHUNKS):
                 halo_arrival(q, side).wait_recv()
                 fwd_copy(q, side).start()
-
-        for side in range(2):
-
-            @pl.when(has[side])
-            def _():
+            for q in range(CHUNKS):
                 fwd_arrival(q, side).wait_recv()
 
-        if q < CHUNKS - 1:
-
-            def add_halo(t, carry):
-                rows = rows_of(t)
-                pre[rows, :] += from_halo(q, cols[rows, :])
-                return carry
-
-            lax.fori_loop(0, tiles, add_halo, 0)
-
-    loads[6].wait()
-
-    def edge_mlp(t, carry):
-        rows = rows_of(t)
-        total = pre[rows, :] + from_halo(CHUNKS - 1, cols[rows, :])
-        mid = silu(total).astype(jnp.bfloat16)
-        normed = layer_norm(dot(mid, ew2[...]))
-        fresh[rows, :] = (edge[rows, :].astype(jnp.float32) + normed).astype(jnp.bfloat16)
-        return carry
-
-    lax.fori_loop(0, tiles, edge_mlp, 0)
+    def edge_mlp(side):
+        def step(t, carry):
+            for k in range(2):
+                rows = rows_of(2 * t + k)
+                hits = picks(cols[rows, :], [4 * side * mesh_rows], 2 * mesh_rows)
+                total = pre[rows, :] + dot(hits, halo[side].reshape(2 * mesh_rows, width))
+                mid = silu(total).astype(jnp.bfloat16)
+                normed = layer_norm(dot(mid, ew2[...]))
+                fresh[rows, :] = (edge[rows, :].astype(jnp.float32) + normed).astype(
+                    jnp.bfloat16
+                )
+            return carry
+
+        lax.fori_loop(0, tiles // 2, step, 0)
 
     def sums(first):
         ids = lax.broadcasted_iota(jnp.int32, (mesh_rows, 128), 0) + first
@@ -332,9 +317,10 @@
         return (block * 2 + c) * mesh_rows
 
     for side in range(2):
+        receive_halo(side)
+        edge_mlp(side)
         pout[side] = sums(block_first(2 * side, peer))
         swap(side).start()
-    for side in range(2):
         acc[...] = sums(block_first(2 * side, col))
         swap(side).wait_recv()
         send[side] = (acc[...] + pin[side]).astype(jnp.bfloat16)
@@ -403,7 +389,6 @@
     grid_rows = grid_lat.shape[0]
     slots = edge_lat.shape[0]
     bf16, f32 = jnp.bfloat16, jnp.float32
-    piece = mesh_rows // CHUNKS
     dma = pltpu.SemaphoreType.DMA
     vmem = pltpu.VMEM
     scratch = [
@@ -412,7 +397,7 @@
         vmem(edge_lat.shape, bf16),
         *[vmem(w.shape, bf16) for w in weights],
         vmem((2, mesh_rows, width), bf16),
-        vmem((CHUNKS, 4, piece, width), bf16),
+        vmem((2, 2, mesh_rows, width), bf16),
         vmem((grid_rows, width), bf16),
         vmem((slots, width), f32),
         vmem((slots, 128), jnp.int32),
@@ -450,7 +435,7 @@
         out_specs=(anywhere, anywhere),
         scratch_shapes=scratch,
         compiler_params=pltpu.CompilerParams(
-            collective_id=0, has_side_effects=True, vmem_limit_bytes=48 * 2**20
+            collective_id=0, has_side_effects=True, vmem_limit_bytes=VMEM_BYTES
         ),
     )(
         *[a.reshape(slots // 128, 128) for a in (edge_src, edge_dst, edge_mask)],

time: 51.8 us -> 37.6 us (0.73); the launches traced: 50.9 us -> 37.4 us
  local copies, waits for them, and re-layouts: 12 us -> 3.93 us
  Pallas kernels: 38.3 us -> 32.8 us
    unnamed x24 -> x2, local copies, waits for them, and re-layouts: 12 us -> 3.93 us
    pallas_call x1, Pallas kernels: 38.3 us -> 32.8 us  [per_device(): pl.pallas_call(functools.partial(kernel, lat_n), out_shape=(jax.ShapeDtyp...]
where the time goes in v2:
time: 37.6 us; the launch traced here: 37.4 us
  Pallas kernels  32.8 us (87%)
  local copies, waits for them, and re-layouts  3.93 us (10%)
  between operations  0.64 us (2%)
    pallas_call x1, Pallas kernels, per_device(): pl.pallas_call(functools.partial(kernel, lat_n), out_shape=(jax.ShapeDtyp...  32.8 us
    unnamed x2, local copies, waits for them, and re-layouts  3.93 us

profile of v2, /device:TPU:8, one launch (start us, length us, event | category | flops | bytes accessed | tf_op | source)
XLA Modules:
  0.0 37.4 jit_solution(2343722524748245158)
XLA Ops:
  0.6 32.8 %shard_map.149 = (bf16[256,512]{1,0:T(8,128)(2,1)}, bf16[1024,512]{1,0:T(8,128)(2,1)}) custom-call(s32[12,128]{1,0:T(8,128)} %bitcast.3, s32[12,128]{1,0:T(8,128)} %bitcast.4, s32[12,128]{1,0:T(8,128)} %bitcast.5, bf16[1024,512]{1,0:T(8,128)(2,1)} %grid_hbm.1, bf16[256,512]{1,0:T(8,128)(2,1)} %mesh_hbm.1, bf16[1536,512]{1,0:T(8,128)(2,1)} %edge_hbm.1, ...), custom_call_target="tpu_custom_call" | custom-call | tf_op jit(solution)/shard_map/pallas_call | solution.py:428
  33.4 1.7 %copy.18 = bf16[256,512]{1,0:T(8,128)(2,1)} copy(bf16[256,512]{1,0:T(8,128)(2,1)} %get-tuple-element.4) | data formatting | bytes 524288
  35.1 2.3 %copy.19 = bf16[1024,512]{1,0:T(8,128)(2,1)} copy(bf16[1024,512]{1,0:T(8,128)(2,1)} %get-tuple-element.5) | data formatting | bytes 2097152

commit v3 on v2

--- a/solution.py
+++ b/solution.py
@@ -8,7 +8,9 @@
 from jax.sharding import PartitionSpec as P
 
 TILE = 256
-CHUNKS = 2
+CHUNKS = 4
+EARLY = 2
+PARTS = 2
 VMEM_BYTES = 63 * 2**20
 MESH = pl.DeviceIdType.MESH
 
@@ -242,31 +244,36 @@
     first_mesh = (band - 1) * 2 * mesh_rows
     live[...] = jnp.where(mask_ref[...] == 1, dst_ref[...] - first_mesh, -1)
 
-    def before_halo(t, carry):
-        rows = rows_of(t)
-        source = spread(src_ref, t)
-        target = spread(dst_ref, t) - first_mesh
-        cols[rows, :] = target
-        total = dot(edge[rows, :], wee[...])
-        total += dot(picks(source, [first_grid], grid_rows), part[...])
-        total += dot(
-            picks(target, [2 * mesh_rows], 2 * mesh_rows),
-            own[...].reshape(2 * mesh_rows, width),
-        )
-        pre[rows, :] = total
+    def before_halo(pair, carry):
+        for t in (2 * pair, 2 * pair + 1):
+            rows = rows_of(t)
+            source = spread(src_ref, t)
+            target = spread(dst_ref, t) - first_mesh
+            cols[rows, :] = target
+            total = dot(edge[rows, :], wee[...])
+            total += dot(picks(source, [first_grid], grid_rows), part[...])
+            total += dot(
+                picks(target, [2 * mesh_rows], 2 * mesh_rows),
+                own[...].reshape(2 * mesh_rows, width),
+            )
+            pre[rows, :] = total
         return carry
 
-    lax.fori_loop(0, tiles, before_halo, 0)
+    lax.fori_loop(0, tiles // 2, before_halo, 0)
 
     send_halo(0)
     loads[6].wait()
 
-    def receive_halo(side):
-        @pl.when(has[side])
-        def _():
-            for q in range(CHUNKS):
+    def forward_halo(side, chunks):
+        @pl.when(has[side])
+        def _():
+            for q in chunks:
                 halo_arrival(q, side).wait_recv()
                 fwd_copy(q, side).start()
+
+    def receive_halo(side):
+        @pl.when(has[side])
+        def _():
             for q in range(CHUNKS):
                 fwd_arrival(q, side).wait_recv()
 
@@ -303,12 +310,14 @@
             device_id_type=MESH,
         )
 
-    def message(side):
-        return pltpu.make_async_remote_copy(
-            src_ref=send.at[side],
-            dst_ref=recv.at[side],
-            send_sem=msg_send.at[side],
-            recv_sem=msg_recv.at[side],
+    some = mesh_rows // PARTS
+
+    def message(side, h):
+        return pltpu.make_async_remote_copy(
+            src_ref=send.at[side, pl.ds(h * some, some)],
+            dst_ref=recv.at[side, pl.ds(h * some, some)],
+            send_sem=msg_send.at[side, h],
+            recv_sem=msg_recv.at[side, h],
             device_id={"lat": toward[side]},
             device_id_type=MESH,
         )
@@ -316,22 +325,35 @@
     def block_first(block, c):
         return (block * 2 + c) * mesh_rows
 
-    for side in range(2):
-        receive_halo(side)
-        edge_mlp(side)
-        pout[side] = sums(block_first(2 * side, peer))
-        swap(side).start()
-        acc[...] = sums(block_first(2 * side, col))
-        swap(side).wait_recv()
-        send[side] = (acc[...] + pin[side]).astype(jnp.bfloat16)
-
-        @pl.when(has[side])
-        def _():
-            message(side).start()
-
+    def send_message(side):
+        @pl.when(has[side])
+        def _():
+            for h in range(PARTS):
+                message(side, h).start()
+
+    forward_halo(0, range(CHUNKS))
+    receive_halo(0)
+    edge_mlp(0)
+    forward_halo(1, range(EARLY))
+    pout[0] = sums(block_first(0, peer))
+    swap(0).start()
+    acc[...] = sums(block_first(0, col))
+    swap(0).wait_recv()
+    send[0] = (acc[...] + pin[0]).astype(jnp.bfloat16)
+    send_message(0)
+
+    forward_halo(1, range(EARLY, CHUNKS))
     pout[2] = sums(block_first(1, peer))
     swap(2).start()
     acc[...] = sums(block_first(1, col))
+    receive_halo(1)
+    edge_mlp(1)
+    pout[1] = sums(block_first(2, peer))
+    swap(1).start()
+    mpre[...] = sums(block_first(2, col))
+    swap(1).wait_recv()
+    send[1] = (mpre[...] + pin[1]).astype(jnp.bfloat16)
+    send_message(1)
 
     for i in (7, 8, 9, 10):
         loads[i].wait()
@@ -350,20 +372,26 @@
     mpre[...] = dot(mesh[...], mw1[:width, :])
     swap(2).wait_recv()
     acc[...] += pin[2]
-    for side in range(2):
-
-        @pl.when(has[1 - side])
-        def _():
-            message(side).wait_recv()
-            acc[...] += recv[side].astype(jnp.float32)
-
-    mid = silu(mpre[...] + dot(acc[...].astype(jnp.bfloat16), mw1[width:, :])).astype(
-        jnp.bfloat16
-    )
-    normed = layer_norm(dot(mid, mw2[...]))
-    mout[...] = (mesh[...].astype(jnp.float32) + normed).astype(jnp.bfloat16)
-    store_mesh = pltpu.make_async_copy(mout, mesh_out, out_sem.at[1])
-    store_mesh.start()
+    stores = []
+    for h in range(PARTS):
+        rows = pl.ds(h * some, some)
+        for side in range(2):
+
+            @pl.when(has[1 - side])
+            def _():
+                message(side, h).wait_recv()
+                acc[rows, :] += recv[side, rows, :].astype(jnp.float32)
+
+        mid = silu(
+            mpre[rows, :] + dot(acc[rows, :].astype(jnp.bfloat16), mw1[width:, :])
+        ).astype(jnp.bfloat16)
+        normed = layer_norm(dot(mid, mw2[...]))
+        mout[rows, :] = (mesh[rows, :].astype(jnp.float32) + normed).astype(jnp.bfloat16)
+        store = pltpu.make_async_copy(
+            mout.at[rows], mesh_out.at[rows], out_sem.at[1 + h]
+        )
+        store.start()
+        stores.append(store)
 
     own_copy.wait_send()
     for i in range(3):
@@ -372,13 +400,15 @@
 
         @pl.when(has[side])
         def _():
-            message(side).wait_send()
+            for h in range(PARTS):
+                message(side, h).wait_send()
             for q in range(CHUNKS):
                 halo_copy(q, side).wait_send()
                 fwd_copy(q, side).wait_send()
 
     store_grid.wait()
-    store_mesh.wait()
+    for store in stores:
+        store.wait()
 
 
 def per_device(lat_n, *args):
@@ -412,7 +442,7 @@
         vmem((2, mesh_rows, width), bf16),
         vmem((mesh_rows, width), f32),
         dma((11,)),
-        dma((2,)),
+        dma((1 + PARTS,)),
         dma((2,)),
         dma((CHUNKS, 2)),
         dma((CHUNKS, 2)),
@@ -420,8 +450,8 @@
         dma((CHUNKS, 2)),
         dma((3,)),
         dma((3,)),
-        dma((2,)),
-        dma((2,)),
+        dma((2, PARTS)),
+        dma((2, PARTS)),
     ]
     in_vmem = pl.BlockSpec(memory_space=pltpu.VMEM)
     anywhere = pl.BlockSpec(memory_space=pl.ANY)

time: 37.6 us -> 38.2 us (1.016)
  Pallas kernels: 32.8 us -> 33.4 us
    pallas_call x1, Pallas kernels: 32.8 us -> 33.4 us  [per_device(): pl.pallas_call(functools.partial(kernel, lat_n), out_shape=(jax.ShapeDtyp...]
where the time goes in v3:
time: 38.2 us; the launch traced here: 37.9 us
  Pallas kernels  33.4 us (87%)
  local copies, waits for them, and re-layouts  3.93 us (10%)
  between operations  0.64 us (2%)
    pallas_call x1, Pallas kernels, per_device(): pl.pallas_call(functools.partial(kernel, lat_n), out_shape=(jax.ShapeDtyp...  33.4 us
    unnamed x2, local copies, waits for them, and re-layouts  3.93 us

profile of v3, /device:TPU:8, one launch (start us, length us, event | category | flops | bytes accessed | tf_op | source)
XLA Modules:
  0.0 37.9 jit_solution(7096807800400839373)
XLA Ops:
  0.6 33.4 %shard_map.149 = (bf16[256,512]{1,0:T(8,128)(2,1)}, bf16[1024,512]{1,0:T(8,128)(2,1)}) custom-call(s32[12,128]{1,0:T(8,128)} %bitcast.3, s32[12,128]{1,0:T(8,128)} %bitcast.4, s32[12,128]{1,0:T(8,128)} %bitcast.5, bf16[1024,512]{1,0:T(8,128)(2,1)} %grid_hbm.1, bf16[256,512]{1,0:T(8,128)(2,1)} %mesh_hbm.1, bf16[1536,512]{1,0:T(8,128)(2,1)} %edge_hbm.1, ...), custom_call_target="tpu_custom_call" | custom-call | tf_op jit(solution)/shard_map/pallas_call | solution.py:458
  34.0 1.7 %copy.18 = bf16[256,512]{1,0:T(8,128)(2,1)} copy(bf16[256,512]{1,0:T(8,128)(2,1)} %get-tuple-element.4) | data formatting | bytes 524288
  35.7 2.3 %copy.19 = bf16[1024,512]{1,0:T(8,128)(2,1)} copy(bf16[1024,512]{1,0:T(8,128)(2,1)} %get-tuple-element.5) | data formatting | bytes 2097152

commit v4 on v3

--- a/solution.py
+++ b/solution.py
@@ -8,9 +8,9 @@
 from jax.sharding import PartitionSpec as P
 
 TILE = 256
-CHUNKS = 4
-EARLY = 2
-PARTS = 2
+CHUNKS = 2
+EARLY = 0
+PARTS = 1
 VMEM_BYTES = 63 * 2**20
 MESH = pl.DeviceIdType.MESH
 

time: 38.2 us -> 37.9 us (level)
  no operation moved by 1% of the time
where the time goes in v4:
time: 37.9 us; the launch traced here: 37.7 us
  Pallas kernels  33.1 us (87%)
  local copies, waits for them, and re-layouts  3.93 us (10%)
  between operations  0.64 us (2%)
    pallas_call x1, Pallas kernels, per_device(): pl.pallas_call(functools.partial(kernel, lat_n), out_shape=(jax.ShapeDtyp...  33.1 us
    unnamed x2, local copies, waits for them, and re-layouts  3.93 us

profile of v4, /device:TPU:8, one launch (start us, length us, event | category | flops | bytes accessed | tf_op | source)
XLA Modules:
  0.0 37.7 jit_solution(3714222663638756221)
XLA Ops:
  0.6 33.1 %shard_map.149 = (bf16[256,512]{1,0:T(8,128)(2,1)}, bf16[1024,512]{1,0:T(8,128)(2,1)}) custom-call(s32[12,128]{1,0:T(8,128)} %bitcast.3, s32[12,128]{1,0:T(8,128)} %bitcast.4, s32[12,128]{1,0:T(8,128)} %bitcast.5, bf16[1024,512]{1,0:T(8,128)(2,1)} %grid_hbm.1, bf16[256,512]{1,0:T(8,128)(2,1)} %mesh_hbm.1, bf16[1536,512]{1,0:T(8,128)(2,1)} %edge_hbm.1, ...), custom_call_target="tpu_custom_call" | custom-call | tf_op jit(solution)/shard_map/pallas_call | solution.py:458
  33.8 1.7 %copy.18 = bf16[256,512]{1,0:T(8,128)(2,1)} copy(bf16[256,512]{1,0:T(8,128)(2,1)} %get-tuple-element.4) | data formatting | bytes 524288
  35.4 2.3 %copy.19 = bf16[1024,512]{1,0:T(8,128)(2,1)} copy(bf16[1024,512]{1,0:T(8,128)(2,1)} %get-tuple-element.5) | data formatting | bytes 2097152

commit v5 on v2

--- a/solution.py
+++ b/solution.py
@@ -319,17 +319,17 @@
     for side in range(2):
         receive_halo(side)
         edge_mlp(side)
-        pout[side] = sums(block_first(2 * side, peer))
+        pout[side] = sums(block_first(2 * side, peer)).astype(jnp.bfloat16)
         swap(side).start()
         acc[...] = sums(block_first(2 * side, col))
         swap(side).wait_recv()
-        send[side] = (acc[...] + pin[side]).astype(jnp.bfloat16)
+        send[side] = (acc[...] + pin[side].astype(jnp.float32)).astype(jnp.bfloat16)
 
         @pl.when(has[side])
         def _():
             message(side).start()
 
-    pout[2] = sums(block_first(1, peer))
+    pout[2] = sums(block_first(1, peer)).astype(jnp.bfloat16)
     swap(2).start()
     acc[...] = sums(block_first(1, col))
 
@@ -349,7 +349,7 @@
 
     mpre[...] = dot(mesh[...], mw1[:width, :])
     swap(2).wait_recv()
-    acc[...] += pin[2]
+    acc[...] += pin[2].astype(jnp.float32)
     for side in range(2):
 
         @pl.when(has[1 - side])
@@ -405,8 +405,8 @@
         vmem((slots, width), bf16),
         vmem((grid_rows, width), bf16),
         vmem((mesh_rows, width), bf16),
-        vmem((3, mesh_rows, width), f32),
-        vmem((3, mesh_rows, width), f32),
+        vmem((3, mesh_rows, width), bf16),
+        vmem((3, mesh_rows, width), bf16),
         vmem((mesh_rows, width), f32),
         vmem((2, mesh_rows, width), bf16),
         vmem((2, mesh_rows, width), bf16),

time: 37.6 us -> 37.5 us (level)
  no operation moved by 1% of the time
where the time goes in v5:
time: 37.5 us; the launch traced here: 37.2 us
  Pallas kernels  32.7 us (87%)
  local copies, waits for them, and re-layouts  3.93 us (10%)
  between operations  0.64 us (2%)
    pallas_call x1, Pallas kernels, per_device(): pl.pallas_call(functools.partial(kernel, lat_n), out_shape=(jax.ShapeDtyp...  32.7 us
    unnamed x2, local copies, waits for them, and re-layouts  3.93 us

profile of v5, /device:TPU:8, one launch (start us, length us, event | category | flops | bytes accessed | tf_op | source)
XLA Modules:
  0.0 37.2 jit_solution(7841304154122785733)
XLA Ops:
  0.6 32.7 %shard_map.149 = (bf16[256,512]{1,0:T(8,128)(2,1)}, bf16[1024,512]{1,0:T(8,128)(2,1)}) custom-call(s32[12,128]{1,0:T(8,128)} %bitcast.3, s32[12,128]{1,0:T(8,128)} %bitcast.4, s32[12,128]{1,0:T(8,128)} %bitcast.5, bf16[1024,512]{1,0:T(8,128)(2,1)} %grid_hbm.1, bf16[256,512]{1,0:T(8,128)(2,1)} %mesh_hbm.1, bf16[1536,512]{1,0:T(8,128)(2,1)} %edge_hbm.1, ...), custom_call_target="tpu_custom_call" | custom-call | tf_op jit(solution)/shard_map/pallas_call | solution.py:428
  33.3 1.7 %copy.18 = bf16[256,512]{1,0:T(8,128)(2,1)} copy(bf16[256,512]{1,0:T(8,128)(2,1)} %get-tuple-element.4) | data formatting | bytes 524288
  35.0 2.3 %copy.19 = bf16[1024,512]{1,0:T(8,128)(2,1)} copy(bf16[1024,512]{1,0:T(8,128)(2,1)} %get-tuple-element.5) | data formatting | bytes 2097152
